TPU v7x, 256 devices: a whole 4x4x8 slice. The times are simulated.
256 devices in a mesh: pipe: 8 (over z), seq: 32 (over y, x, core).
Axes of the slice: x: 4, y: 4, z: 8, core: 2. Of those that a mesh axis runs over, the one named last changes fastest.
Arguments:
- section_input: bfloat16 [8, 8192, 1024], P('pipe', 'seq'), may hold values from -6 to 6
- saved_input: bfloat16 [8, 8192, 1024], P('pipe', 'seq'), may hold values from -6 to 6
- grad_output: bfloat16 [8, 8192, 1024], P('pipe', 'seq'), may hold values from -6 to 6
- w_qkv: bfloat16 [8, 3072, 1024], P('pipe'), may hold values from -0.1875 to 0.1875
- w_out: bfloat16 [8, 1024, 1024], P('pipe'), may hold values from -0.75 to 0.75
- tile_cluster: int32 [64], replicated, may hold values from 0 to 31, as said below
Outputs:
- next_input: bfloat16 [8, 8192, 1024], P('pipe', 'seq')
- grad_input: bfloat16 [8, 8192, 1024], P('pipe', 'seq')
Inputs may be any that keep to these rules, and one draw needn't show every extreme that they name: `tile_cluster`: each of the 32 ids names between 1 and 3 tiles, and some id names exactly 3. The id of tile i leaves the remainder i % 4 when divided by 4.
All inputs are finite; a program needn't handle non-finite values.
Results may differ from a plain program's by a relative error of at most 0.007.
Values may be sent and summed in bfloat16 or wider, within the bound.
A program may use at most 128 MiB of HBM per device.

v0:
```python
import jax
import jax.numpy as jnp
from jax import lax
from jax.experimental import pallas as pl
from jax.experimental.pallas import tpu as pltpu
from jax.sharding import PartitionSpec as P

MESH = pl.DeviceIdType.MESH
HEADS = 8
HD = 128
TILE = 128
D = 1024
GROUP = 16
CAP = 3
LIST = 8
EPS = 1e-05
FACTOR = HD ** (-0.5)
F32 = jnp.float32
BF16 = jnp.bfloat16


def nt(a, b):
    return lax.dot_general(a, b, (((1,), (1,)), ((), ())), preferred_element_type=F32)


def tn(a, b):
    return lax.dot_general(a, b, (((0,), (0,)), ((), ())), preferred_element_type=F32)


def nn(a, b):
    return jnp.dot(a, b, preferred_element_type=F32)


def inv_rms(u):
    return lax.rsqrt(jnp.mean(u * u, axis=-1, keepdims=True) + EPS)


def ring_order(i):
    return (1 + 2 * i - 3 * (i // 2)) % 4


def landed(ref, sem):
    pltpu.make_async_copy(ref, ref, sem).wait()


def kernel(
    tc_ref, x_hbm, xs_hbm, g_hbm, wq_hbm, wo_hbm,
    on_hbm, og_hbm,
    wq, wo, xin, xn, mixed, sf, sb, rf, rb, dst, ptm, fo, fr, bo, br, att, gm, gn, res,
    lists,
    w_sem, ex_ss, ex_rs, f_ss, f_rs, b_ss, b_rs, d_ss, d_rs,
    fo_ss, fo_rs, dq_ss, dq_rs, dkv_ss, dkv_rs, pf_ss, pf_rs, pb_ss, pb_rs,
):
    z = lax.axis_index("pipe")
    s = lax.axis_index("seq")
    y = s // 8
    x = (s // 2) % 4
    c = s % 2

    def seq_of(xx, yy, cc):
        return (yy * 4 + xx) * 2 + cc

    def f_dev(h):
        return (z, seq_of(x, h // 2, h % 2))

    def b_dev(h):
        return (z, seq_of(h // 2, y, h % 2))

    f_me = y * 2 + c
    b_me = x * 2 + c
    up = (z + 1) % 8
    down = (z + 7) % 8

    w_copies = [
        pltpu.make_async_copy(wq_hbm.at[0], wq, w_sem.at[0]),
        pltpu.make_async_copy(wo_hbm.at[0], wo, w_sem.at[1]),
    ]
    for copy in w_copies:
        copy.start()

    barrier = pltpu.get_barrier_semaphore()

    def greet(dev):
        pl.semaphore_signal(barrier, inc=1, device_id=dev, device_id_type=MESH)

    for i in range(1, 8):
        greet(f_dev((f_me + i) % 8))
    for i in range(2, 8):
        greet(b_dev((2 * x + i) % 8))
    for k in range(2):
        for zz in (up, down):
            greet((zz, seq_of(2 * c + k, y, x // 2)))
            greet((zz, seq_of(x, 2 * c + k, y // 2)))
    pl.semaphore_wait(barrier, 21)

    def exchange(t, src_hbm, j, forward):
        other = 2 * c + j
        own = x if forward else y
        dev = (z, seq_of(other, y, x // 2) if forward else seq_of(x, other, y // 2))
        src = src_hbm.at[0, pl.ds(j * TILE, TILE)]
        dst_ref = xin.at[t, pl.ds((own % 2) * TILE, TILE)]
        recv = ex_rs.at[t, own % 2]

        @pl.when(own == other)
        def _():
            pltpu.make_async_copy(src, dst_ref, recv).start()

        @pl.when(own != other)
        def _():
            pltpu.make_async_remote_copy(
                src_ref=src, dst_ref=dst_ref, send_sem=ex_ss.at[t, j], recv_sem=recv,
                device_id=dev, device_id_type=MESH,
            ).start()

    def exchange_sent(t, j, forward):
        own = x if forward else y

        @pl.when(own != 2 * c + j)
        def _():
            landed(xin.at[t, pl.ds(j * TILE, TILE)], ex_ss.at[t, j])

    def exchange_wait(t):
        for k in range(2):
            landed(xin.at[t, pl.ds(k * TILE, TILE)], ex_rs.at[t, k])

    for j in range(2):
        exchange(1, xs_hbm, j, False)
        exchange(0, x_hbm, j, True)
    for j in range(2):
        exchange(2, g_hbm, j, False)

    def fill(base, tile_of):
        ids = [tc_ref[tile_of(q)] for q in range(GROUP)]

        def one(q, carry):
            own_id = tc_ref[tile_of(q)]
            count = jnp.int32(0)
            rank = jnp.int32(0)
            members = [jnp.int32(GROUP)] * CAP
            for p in range(GROUP):
                same = ids[p] == own_id
                members = [
                    jnp.where(same & (count == k), p, members[k]) for k in range(CAP)
                ]
                rank = rank + jnp.where(same & (p < q), 1, 0)
                count = count + jnp.where(same, 1, 0)
            row = base + q * LIST
            for k in range(CAP):
                lists[row + k] = members[k]
            lists[row + 3] = jnp.minimum(rank, CAP - 1)
            lists[row + 4] = count
            return carry

        lax.fori_loop(0, GROUP, one, 0)

    fill(0, lambda q: 4 * q + x)
    fill(GROUP * LIST, lambda q: 4 * ((q % 4) * 4 + q // 4) + y)

    zero = jnp.zeros((TILE, HD), BF16)
    for t in range(3):
        rf[t, GROUP] = zero
    for t in range(4):
        rb[t, GROUP] = zero
    for k in range(CAP):
        dst[GROUP, k] = zero
        ptm[GROUP, k] = zero

    def ship(src, dst_ref, send_sem, recv_sem, dev, is_self):
        @pl.when(is_self)
        def _():
            pltpu.make_async_copy(src, dst_ref, recv_sem).start()

        @pl.when(jnp.logical_not(is_self))
        def _():
            pltpu.make_async_remote_copy(
                src_ref=src, dst_ref=dst_ref, send_sem=send_sem, recv_sem=recv_sem,
                device_id=dev, device_id_type=MESH,
            ).start()

    def normalise(t, slot):
        for k in range(2):
            rows = pl.ds(k * TILE, TILE)
            u = xin[t, rows].astype(F32)
            xn[slot, rows] = (u * inv_rms(u)).astype(BF16)

    exchange_wait(1)
    normalise(1, 1)
    w_copies[0].wait()

    def b_project(i, carry):
        a = (x + ring_order(i)) % 4
        rows = xn[1]
        for t in range(3):
            m = nt(rows, wq[pl.ds(pl.multiple_of(t * D + a * 256, 256), 256), :])
            for cc in range(2):
                u = m[:, cc * HD : (cc + 1) * HD]
                h = 2 * a + cc
                if t < 2:
                    mixed[t, h] = u
                    u = u * inv_rms(u)
                sb[h, t] = u.astype(BF16).reshape(2, TILE, HD)
        for cc in range(2):
            h = 2 * a + cc
            ship(
                sb.at[h, pl.ds(0, 3)], rb.at[pl.ds(0, 3), pl.ds(2 * b_me, 2)],
                b_ss.at[h], b_rs.at[b_me], b_dev(h), h == b_me,
            )
        return carry

    lax.fori_loop(0, 4, b_project, 0)

    exchange_wait(0)
    normalise(0, 0)

    def f_project(i, carry):
        a = (y + ring_order(i)) % 4
        rows = xn[0]
        for t in range(3):
            m = nt(rows, wq[pl.ds(pl.multiple_of(t * D + a * 256, 256), 256), :])
            for cc in range(2):
                u = m[:, cc * HD : (cc + 1) * HD]
                if t < 2:
                    u = u * inv_rms(u)
                sf[2 * a + cc, t] = u.astype(BF16).reshape(2, TILE, HD)
        for cc in range(2):
            h = 2 * a + cc
            ship(
                sf.at[h], rf.at[:, pl.ds(2 * f_me, 2)],
                f_ss.at[h], f_rs.at[f_me], f_dev(h), h == f_me,
            )
        return carry

    lax.fori_loop(0, 4, f_project, 0)

    exchange_wait(2)
    w_copies[1].wait()

    def d_project(i, carry):
        a = (x + ring_order(i)) % 4
        m = nt(xin[2], wo[pl.ds(pl.multiple_of(a * 256, 256), 256), :])
        for cc in range(2):
            h = 2 * a + cc
            sb[h, 3] = m[:, cc * HD : (cc + 1) * HD].astype(BF16).reshape(2, TILE, HD)
            ship(
                sb.at[h, 3], rb.at[3, pl.ds(2 * b_me, 2)],
                d_ss.at[h], d_rs.at[b_me], b_dev(h), h == b_me,
            )
        return carry

    lax.fori_loop(0, 4, d_project, 0)

    def member_row(base, q):
        row = base + q * LIST
        return [lists[row + k] for k in range(5)]

    def weights_of(queries, keys, count):
        e = jnp.exp(nt(keys, queries) * FACTOR)
        parts = [e[:TILE]]
        for k in range(1, CAP):
            parts.append(e[k * TILE : (k + 1) * TILE] * jnp.where(count > k, 1.0, 0.0))
        e = jnp.concatenate(parts, axis=0)
        return e * (1.0 / jnp.sum(e, axis=0, keepdims=True))

    def stacked(ref, t, members):
        return jnp.concatenate([ref[t, members[k]] for k in range(CAP)], axis=0)

    for p in range(8):
        landed(rb.at[pl.ds(0, 3), pl.ds(2 * p, 2)], b_rs.at[p])
        landed(rb.at[3, pl.ds(2 * p, 2)], d_rs.at[p])

    def b_first(i, carry):
        p = ((x + ring_order(i // 2)) % 4) * 2 + i % 2
        for k in range(2):
            q = 2 * p + k
            m0, m1, m2, rank, count = member_row(GROUP * LIST, q)
            members = (m0, m1, m2)
            queries, grads = rb[0, q], rb[3, q]
            keys = stacked(rb, 1, members)
            values = stacked(rb, 2, members)
            soft = weights_of(queries, keys, count)
            low = soft.astype(BF16)
            grad_soft = nt(values, grads)
            delta = jnp.sum(low.astype(F32) * grad_soft, axis=0, keepdims=True)
            grad_scores = (soft * (grad_soft - delta)).astype(BF16)
            ptm[q] = low.reshape(CAP, TILE, HD)
            dst[q] = grad_scores.reshape(CAP, TILE, HD)
            bo[0, p, k] = (tn(grad_scores, keys) * FACTOR).astype(BF16)
        ship(bo.at[0, p], br.at[0, b_me], dq_ss.at[p], dq_rs.at[b_me], b_dev(p), p == b_me)
        return carry

    lax.fori_loop(0, 8, b_first, 0)

    def b_second(i, carry):
        p = ((x + ring_order(i // 2)) % 4) * 2 + i % 2
        for k in range(2):
            q = 2 * p + k
            m0, m1, m2, rank, count = member_row(GROUP * LIST, q)
            members = (m0, m1, m2)
            ds = jnp.concatenate([dst[m, rank] for m in members], axis=1)
            pt = jnp.concatenate([ptm[m, rank] for m in members], axis=1)
            bo[1, p, k] = (nn(ds, stacked(rb, 0, members)) * FACTOR).astype(BF16)
            bo[2, p, k] = nn(pt, stacked(rb, 3, members)).astype(BF16)
        ship(
            bo.at[pl.ds(1, 2), p], br.at[pl.ds(1, 2), b_me],
            dkv_ss.at[p], dkv_rs.at[b_me], b_dev(p), p == b_me,
        )
        return carry

    lax.fori_loop(0, 8, b_second, 0)

    for p in range(8):
        landed(rf.at[:, pl.ds(2 * p, 2)], f_rs.at[p])

    def f_attend(i, carry):
        p = ((y + ring_order(i // 2)) % 4) * 2 + i % 2
        for k in range(2):
            q = 2 * p + k
            m0, m1, m2, rank, count = member_row(0, q)
            members = (m0, m1, m2)
            low = weights_of(rf[0, q], stacked(rf, 1, members), count).astype(BF16)
            fo[p, k] = tn(low, stacked(rf, 2, members)).astype(BF16)
        ship(fo.at[p], fr.at[f_me], fo_ss.at[p], fo_rs.at[f_me], f_dev(p), p == f_me)
        return carry

    lax.fori_loop(0, 8, f_attend, 0)

    for h in range(HEADS):
        landed(fr.at[h], fo_rs.at[h])
        att[:, h * HD : (h + 1) * HD] = fr[h].reshape(2 * TILE, HD)

    def pipe_copy(result, k, out, dev, slot, send_sem, recv_sem):
        return pltpu.make_async_remote_copy(
            src_ref=res.at[result, pl.ds(k * TILE, TILE)],
            dst_ref=out.at[0, pl.ds(slot * TILE, TILE)],
            send_sem=send_sem.at[k], recv_sem=recv_sem.at[slot],
            device_id=dev, device_id_type=MESH,
        )

    def f_out(n, carry):
        cols = pl.ds(pl.multiple_of(n * 256, 256), 256)
        total = xin[0, :, cols].astype(F32) + nn(att[...], wo[:, cols])
        res[0, :, cols] = total.astype(BF16)
        return carry

    lax.fori_loop(0, 4, f_out, 0)

    @pl.when(z != 7)
    def _():
        for k in range(2):
            pipe_copy(0, k, on_hbm, (up, seq_of(2 * c + k, y, x // 2)), x % 2, pf_ss, pf_rs).start()

    def b_jacobian(i, carry):
        h = ((x + ring_order(i // 2)) % 4) * 2 + i % 2
        landed(br.at[0, h], dq_rs.at[h])
        landed(br.at[pl.ds(1, 2), h], dkv_rs.at[h])
        for t in range(2):
            u = mixed[t, h]
            r = inv_rms(u)
            unit = u * r
            g = br[t, h].reshape(2 * TILE, HD).astype(F32)
            back = r * (g - unit * jnp.mean(unit * g, axis=-1, keepdims=True))
            gm[:, pl.ds(pl.multiple_of(t * D + h * HD, HD), HD)] = back.astype(BF16)
        gm[:, pl.ds(pl.multiple_of(2 * D + h * HD, HD), HD)] = br[2, h].reshape(2 * TILE, HD)
        return carry

    lax.fori_loop(0, 8, b_jacobian, 0)

    def b_normed(n, carry):
        cols = pl.ds(pl.multiple_of(n * 256, 256), 256)
        gn[:, cols] = nn(gm[...], wq[:, cols])
        return carry

    lax.fori_loop(0, 4, b_normed, 0)

    for k in range(2):
        rows = pl.ds(k * TILE, TILE)
        u = xin[1, rows].astype(F32)
        r = inv_rms(u)
        unit = u * r
        g = gn[rows]
        back = r * (g - unit * jnp.mean(unit * g, axis=-1, keepdims=True))
        res[1, rows] = (xin[2, rows].astype(F32) + back).astype(BF16)

        @pl.when(z != 0)
        def _():
            pipe_copy(1, k, og_hbm, (down, seq_of(x, 2 * c + k, y // 2)), y % 2, pb_ss, pb_rs).start()

    for j in range(2):
        exchange_sent(0, j, True)
        exchange_sent(1, j, False)
        exchange_sent(2, j, False)

    def drain(h, carry):
        @pl.when(h != b_me)
        def _():
            landed(sb.at[h, pl.ds(0, 3)], b_ss.at[h])
            landed(sb.at[h, 3], d_ss.at[h])
            landed(bo.at[0, h], dq_ss.at[h])
            landed(bo.at[pl.ds(1, 2), h], dkv_ss.at[h])

        @pl.when(h != f_me)
        def _():
            landed(sf.at[h], f_ss.at[h])
            landed(fo.at[h], fo_ss.at[h])

        return carry

    lax.fori_loop(0, 8, drain, 0)

    @pl.when(z != 7)
    def _():
        for k in range(2):
            landed(res.at[0, pl.ds(k * TILE, TILE)], pf_ss.at[k])

    @pl.when(z != 0)
    def _():
        for k in range(2):
            landed(res.at[1, pl.ds(k * TILE, TILE)], pb_ss.at[k])
            landed(on_hbm.at[0, pl.ds(k * TILE, TILE)], pf_rs.at[k])

    @pl.when(z != 7)
    def _():
        for k in range(2):
            landed(og_hbm.at[0, pl.ds(k * TILE, TILE)], pb_rs.at[k])


def per_device(section_input, saved_input, grad_output, w_qkv, w_out, tile_cluster):
    any_spec = pl.BlockSpec(memory_space=pl.ANY)
    dma = pltpu.SemaphoreType.DMA
    block = jax.ShapeDtypeStruct((1, 2 * TILE, D), BF16)
    ahead, back = pl.pallas_call(
        kernel,
        out_shape=(block, block),
        in_specs=[pl.BlockSpec(memory_space=pltpu.SMEM)] + [any_spec] * 5,
        out_specs=(any_spec, any_spec),
        scratch_shapes=[
            pltpu.VMEM((3 * D, D), BF16),
            pltpu.VMEM((D, D), BF16),
            pltpu.VMEM((3, 2 * TILE, D), BF16),
            pltpu.VMEM((2, 2 * TILE, D), BF16),
            pltpu.VMEM((2, HEADS, 2 * TILE, HD), F32),
            pltpu.VMEM((HEADS, 3, 2, TILE, HD), BF16),
            pltpu.VMEM((HEADS, 4, 2, TILE, HD), BF16),
            pltpu.VMEM((3, GROUP + 1, TILE, HD), BF16),
            pltpu.VMEM((4, GROUP + 1, TILE, HD), BF16),
            pltpu.VMEM((GROUP + 1, CAP, TILE, HD), BF16),
            pltpu.VMEM((GROUP + 1, CAP, TILE, HD), BF16),
            pltpu.VMEM((HEADS, 2, TILE, HD), BF16),
            pltpu.VMEM((HEADS, 2, TILE, HD), BF16),
            pltpu.VMEM((3, HEADS, 2, TILE, HD), BF16),
            pltpu.VMEM((3, HEADS, 2, TILE, HD), BF16),
            pltpu.VMEM((2 * TILE, D), BF16),
            pltpu.VMEM((2 * TILE, 3 * D), BF16),
            pltpu.VMEM((2 * TILE, D), F32),
            pltpu.VMEM((2, 2 * TILE, D), BF16),
            pltpu.SMEM((2 * GROUP * LIST,), jnp.int32),
            dma((2,)), dma((3, 2)), dma((3, 2)),
            dma((8,)), dma((8,)), dma((8,)), dma((8,)), dma((8,)), dma((8,)),
            dma((8,)), dma((8,)), dma((8,)), dma((8,)), dma((8,)), dma((8,)),
            dma((2,)), dma((2,)), dma((2,)), dma((2,)),
        ],
        compiler_params=pltpu.CompilerParams(
            collective_id=0, has_side_effects=True, vmem_limit_bytes=56 * 2**20
        ),
    )(tile_cluster, section_input, saved_input, grad_output, w_qkv, w_out)
    z = lax.axis_index("pipe")
    nothing = jnp.zeros((), BF16)
    return (
        jnp.where(z == 0, nothing, ahead),
        jnp.where(z == lax.axis_size("pipe") - 1, nothing, back),
    )


def solution(mesh):
    return jax.shard_map(
        per_device,
        mesh=mesh,
        in_specs=(
            P("pipe", "seq", None),
            P("pipe", "seq", None),
            P("pipe", "seq", None),
            P("pipe", None, None),
            P("pipe", None, None),
            P(),
        ),
        out_specs=(P("pipe", "seq", None), P("pipe", "seq", None)),
        check_vma=False,
    )
```

profile of v0, /device:TPU:91, one launch (start us, length us, event | category | flops | bytes accessed | tf_op | source)
XLA Modules:
  0.0 86.3 jit_solution(7609672489038017609)
XLA Ops:
  0.6 83.4 %shard_map.77 = (bf16[1,256,1024]{2,1,0:T(8,128)(2,1)}, bf16[1,256,1024]{2,1,0:T(8,128)(2,1)}) custom-call(s32[64]{0:T(128)} %tc_ref.1, bf16[1,256,1024]{2,1,0:T(8,128)(2,1)} %x_hbm.1, bf16[1,256,1024]{2,1,0:T(8,128)(2,1)} %xs_hbm.1, bf16[1,256,1024]{2,1,0:T(8,128)(2,1)} %g_hbm.1, bf16[1,3072,1024]{2,1,0:T(8,128)(2,1)} %wq_hbm.1, bf16[1,1024,1024]{2,1,0:T(8,128)(2,1)} %wo_hbm.1), custom_call_target="tpu_custom_call" | custom-call | tf_op jit(solution)/shard_map/pallas_call | solution.py:431
  84.1 2.2 %broadcast_select_fusion = (bf16[1,256,1024]{2,1,0:T(8,128)(2,1)}, bf16[1,256,1024]{2,1,0:T(8,128)(2,1)}) fusion(bf16[1,256,1024]{2,1,0:T(8,128)(2,1)} %get-tuple-element.5, pred[]{:T(512)S(6)} %eq.7, bf16[1,256,1024]{2,1,0:T(8,128)(2,1)} %get-tuple-element.4, pred[]{:T(512)S(6)} %eq.6), kind=kLoop, calls=%fused_computation | loop fusion | flops 524288 | bytes 2097154 | tf_op jit(solution)/shard_map/jit(_where)/select_n | solution.py:470
where the time goes:
time: 86.5 us; the launch traced here: 86.3 us
  Pallas kernels  83.4 us (96%)
  other arithmetic  2.25 us (3%)
    pallas_call x1, Pallas kernels, per_device(): pl.pallas_call(kernel, out_shape=(block, block), in_specs=[pl.BlockSpec(m...  83.4 us
    select_n x1, other arithmetic, per_device(): jnp.where(z == lax.axis_size('pipe') - 1, nothing, back)  2.25 us

commit v1 on v0

--- a/solution.py
+++ b/solution.py
@@ -46,7 +46,7 @@
 def kernel(
     tc_ref, x_hbm, xs_hbm, g_hbm, wq_hbm, wo_hbm,
     on_hbm, og_hbm,
-    wq, wo, xin, xn, mixed, sf, sb, rf, rb, dst, ptm, fo, fr, bo, br, att, gm, gn, res,
+    wq, wo, xin, xn, mixed, sf, sb, rf, rb, rd, soft, dst, ptm, fo, fr, bo, br, att, gm, gn, res,
     lists,
     w_sem, ex_ss, ex_rs, f_ss, f_rs, b_ss, b_rs, d_ss, d_rs,
     fo_ss, fo_rs, dq_ss, dq_rs, dkv_ss, dkv_rs, pf_ss, pf_rs, pb_ss, pb_rs,
@@ -98,8 +98,9 @@
         own = x if forward else y
         dev = (z, seq_of(other, y, x // 2) if forward else seq_of(x, other, y // 2))
         src = src_hbm.at[0, pl.ds(j * TILE, TILE)]
-        dst_ref = xin.at[t, pl.ds((own % 2) * TILE, TILE)]
-        recv = ex_rs.at[t, own % 2]
+        slot = (own + j) % 2
+        dst_ref = xin.at[t, pl.ds(slot * TILE, TILE)]
+        recv = ex_rs.at[t, slot]
 
         @pl.when(own == other)
         def _():
@@ -126,8 +127,11 @@
     for j in range(2):
         exchange(1, xs_hbm, j, False)
         exchange(0, x_hbm, j, True)
-    for j in range(2):
-        exchange(2, g_hbm, j, False)
+    def f_source(k):
+        return 2 * c + (k + x) % 2
+
+    def b_source(k):
+        return 2 * c + (k + y) % 2
 
     def fill(base, tile_of):
         ids = [tc_ref[tile_of(q)] for q in range(GROUP)]
@@ -153,14 +157,14 @@
 
         lax.fori_loop(0, GROUP, one, 0)
 
-    fill(0, lambda q: 4 * q + x)
-    fill(GROUP * LIST, lambda q: 4 * ((q % 4) * 4 + q // 4) + y)
+    fill(0, lambda q: 4 * ((q // 2) * 2 + (q + x) % 2) + x)
+    fill(GROUP * LIST, lambda q: 4 * ((((q // 2) % 2) * 2 + (q + y) % 2) * 4 + q // 4) + y)
 
     zero = jnp.zeros((TILE, HD), BF16)
     for t in range(3):
         rf[t, GROUP] = zero
-    for t in range(4):
         rb[t, GROUP] = zero
+    rd[GROUP] = zero
     for k in range(CAP):
         dst[GROUP, k] = zero
         ptm[GROUP, k] = zero
@@ -184,6 +188,8 @@
             xn[slot, rows] = (u * inv_rms(u)).astype(BF16)
 
     exchange_wait(1)
+    for j in range(2):
+        exchange(2, g_hbm, j, False)
     normalise(1, 1)
     w_copies[0].wait()
 
@@ -202,7 +208,7 @@
         for cc in range(2):
             h = 2 * a + cc
             ship(
-                sb.at[h, pl.ds(0, 3)], rb.at[pl.ds(0, 3), pl.ds(2 * b_me, 2)],
+                sb.at[h, pl.ds(0, 3)], rb.at[:, pl.ds(2 * b_me, 2)],
                 b_ss.at[h], b_rs.at[b_me], b_dev(h), h == b_me,
             )
         return carry
@@ -242,7 +248,7 @@
             h = 2 * a + cc
             sb[h, 3] = m[:, cc * HD : (cc + 1) * HD].astype(BF16).reshape(2, TILE, HD)
             ship(
-                sb.at[h, 3], rb.at[3, pl.ds(2 * b_me, 2)],
+                sb.at[h, 3], rd.at[pl.ds(2 * b_me, 2)],
                 d_ss.at[h], d_rs.at[b_me], b_dev(h), h == b_me,
             )
         return carry
@@ -254,136 +260,181 @@
         return [lists[row + k] for k in range(5)]
 
     def weights_of(queries, keys, count):
-        e = jnp.exp(nt(keys, queries) * FACTOR)
-        parts = [e[:TILE]]
+        e = jnp.exp(nt(queries, keys) * FACTOR)
+        parts = [e[:, :TILE]]
         for k in range(1, CAP):
-            parts.append(e[k * TILE : (k + 1) * TILE] * jnp.where(count > k, 1.0, 0.0))
-        e = jnp.concatenate(parts, axis=0)
-        return e * (1.0 / jnp.sum(e, axis=0, keepdims=True))
+            parts.append(e[:, k * TILE : (k + 1) * TILE] * jnp.where(count > k, 1.0, 0.0))
+        total = jnp.sum(parts[0] + parts[1] + parts[2], axis=1, keepdims=True)
+        return jnp.concatenate(parts, axis=1) * (1.0 / total)
 
     def stacked(ref, t, members):
-        return jnp.concatenate([ref[t, members[k]] for k in range(CAP)], axis=0)
+        return jnp.concatenate([ref[t, m] for m in members], axis=0)
 
     for p in range(8):
-        landed(rb.at[pl.ds(0, 3), pl.ds(2 * p, 2)], b_rs.at[p])
-        landed(rb.at[3, pl.ds(2 * p, 2)], d_rs.at[p])
+        landed(rb.at[:, pl.ds(2 * p, 2)], b_rs.at[p])
+
+    def b_soft(i, carry):
+        for k in range(4):
+            q = 4 * i + k
+            m0, m1, m2, rank, count = member_row(GROUP * LIST, q)
+            soft[q] = weights_of(rb[0, q], stacked(rb, 1, (m0, m1, m2)), count)
+        return carry
+
+    lax.fori_loop(0, 4, b_soft, 0)
+
+    for p in range(8):
+        landed(rd.at[pl.ds(2 * p, 2)], d_rs.at[p])
 
     def b_first(i, carry):
-        p = ((x + ring_order(i // 2)) % 4) * 2 + i % 2
-        for k in range(2):
+        a = (x + ring_order(i)) % 4
+        for k in range(4):
+            p = 2 * a + k // 2
+            q = 4 * a + k
+            m0, m1, m2, rank, count = member_row(GROUP * LIST, q)
+            members = (m0, m1, m2)
+            grad_soft = nt(rd[q], stacked(rb, 2, members))
+            weights = soft[q]
+            low = weights.astype(BF16)
+            delta = jnp.sum(low.astype(F32) * grad_soft, axis=1, keepdims=True)
+            grad_scores = (weights * (grad_soft - delta)).astype(BF16)
+            for n in range(CAP):
+                ptm[q, n] = low[:, n * TILE : (n + 1) * TILE]
+                dst[q, n] = grad_scores[:, n * TILE : (n + 1) * TILE]
+            bo[0, p, k % 2] = (nn(grad_scores, stacked(rb, 1, members)) * FACTOR).astype(BF16)
+        for cc in range(2):
+            p = 2 * a + cc
+            ship(bo.at[0, p], br.at[0, b_me], dq_ss.at[p], dq_rs.at[b_me], b_dev(p), p == b_me)
+        return carry
+
+    lax.fori_loop(0, 4, b_first, 0)
+
+    for p in range(8):
+        landed(rf.at[:, pl.ds(2 * p, 2)], f_rs.at[p])
+
+    def f_attend(i, carry):
+        a = (y + ring_order(i)) % 4
+        for k in range(4):
+            q = 4 * a + k
+            m0, m1, m2, rank, count = member_row(0, q)
+            members = (m0, m1, m2)
+            low = weights_of(rf[0, q], stacked(rf, 1, members), count).astype(BF16)
+            fo[2 * a + k // 2, k % 2] = nn(low, stacked(rf, 2, members)).astype(BF16)
+        for cc in range(2):
+            p = 2 * a + cc
+            ship(fo.at[p], fr.at[f_me], fo_ss.at[p], fo_rs.at[f_me], f_dev(p), p == f_me)
+        return carry
+
+    lax.fori_loop(0, 4, f_attend, 0)
+
+    def b_second(i, carry):
+        k = i // 4
+        a = (x + ring_order(i % 4)) % 4
+        for cc in range(2):
+            p = 2 * a + cc
             q = 2 * p + k
             m0, m1, m2, rank, count = member_row(GROUP * LIST, q)
             members = (m0, m1, m2)
-            queries, grads = rb[0, q], rb[3, q]
-            keys = stacked(rb, 1, members)
-            values = stacked(rb, 2, members)
-            soft = weights_of(queries, keys, count)
-            low = soft.astype(BF16)
-            grad_soft = nt(values, grads)
-            delta = jnp.sum(low.astype(F32) * grad_soft, axis=0, keepdims=True)
-            grad_scores = (soft * (grad_soft - delta)).astype(BF16)
-            ptm[q] = low.reshape(CAP, TILE, HD)
-            dst[q] = grad_scores.reshape(CAP, TILE, HD)
-            bo[0, p, k] = (tn(grad_scores, keys) * FACTOR).astype(BF16)
-        ship(bo.at[0, p], br.at[0, b_me], dq_ss.at[p], dq_rs.at[b_me], b_dev(p), p == b_me)
-        return carry
-
-    lax.fori_loop(0, 8, b_first, 0)
-
-    def b_second(i, carry):
-        p = ((x + ring_order(i // 2)) % 4) * 2 + i % 2
-        for k in range(2):
-            q = 2 * p + k
-            m0, m1, m2, rank, count = member_row(GROUP * LIST, q)
-            members = (m0, m1, m2)
-            ds = jnp.concatenate([dst[m, rank] for m in members], axis=1)
-            pt = jnp.concatenate([ptm[m, rank] for m in members], axis=1)
-            bo[1, p, k] = (nn(ds, stacked(rb, 0, members)) * FACTOR).astype(BF16)
-            bo[2, p, k] = nn(pt, stacked(rb, 3, members)).astype(BF16)
-        ship(
-            bo.at[pl.ds(1, 2), p], br.at[pl.ds(1, 2), b_me],
-            dkv_ss.at[p], dkv_rs.at[b_me], b_dev(p), p == b_me,
-        )
+            ds = jnp.concatenate([dst[m, rank] for m in members], axis=0)
+            pt = jnp.concatenate([ptm[m, rank] for m in members], axis=0)
+            bo[1, p, k] = (tn(ds, stacked(rb, 0, members)) * FACTOR).astype(BF16)
+            bo[2, p, k] = tn(pt, jnp.concatenate([rd[m] for m in members], axis=0)).astype(BF16)
+        for cc in range(2):
+            p = 2 * a + cc
+            ship(
+                bo.at[pl.ds(1, 2), p, k], br.at[pl.ds(1, 2), b_me, k],
+                dkv_ss.at[k, p], dkv_rs.at[k, b_me], b_dev(p), p == b_me,
+            )
         return carry
 
     lax.fori_loop(0, 8, b_second, 0)
-
-    for p in range(8):
-        landed(rf.at[:, pl.ds(2 * p, 2)], f_rs.at[p])
-
-    def f_attend(i, carry):
-        p = ((y + ring_order(i // 2)) % 4) * 2 + i % 2
-        for k in range(2):
-            q = 2 * p + k
-            m0, m1, m2, rank, count = member_row(0, q)
-            members = (m0, m1, m2)
-            low = weights_of(rf[0, q], stacked(rf, 1, members), count).astype(BF16)
-            fo[p, k] = tn(low, stacked(rf, 2, members)).astype(BF16)
-        ship(fo.at[p], fr.at[f_me], fo_ss.at[p], fo_rs.at[f_me], f_dev(p), p == f_me)
-        return carry
-
-    lax.fori_loop(0, 8, f_attend, 0)
 
     for h in range(HEADS):
         landed(fr.at[h], fo_rs.at[h])
         att[:, h * HD : (h + 1) * HD] = fr[h].reshape(2 * TILE, HD)
 
-    def pipe_copy(result, k, out, dev, slot, send_sem, recv_sem):
-        return pltpu.make_async_remote_copy(
+    def f_result(k):
+        rows = pl.ds(k * TILE, TILE)
+
+        def columns(n, carry):
+            cols = pl.ds(pl.multiple_of(n * 256, 256), 256)
+            total = xin[0, rows, cols].astype(F32) + nn(att[rows], wo[:, cols])
+            res[0, rows, cols] = total.astype(BF16)
+            return carry
+
+        lax.fori_loop(0, 4, columns, 0)
+
+    def pipe_start(result, k, out, dev, slot, send_sem, recv_sem):
+        pltpu.make_async_remote_copy(
             src_ref=res.at[result, pl.ds(k * TILE, TILE)],
             dst_ref=out.at[0, pl.ds(slot * TILE, TILE)],
             send_sem=send_sem.at[k], recv_sem=recv_sem.at[slot],
             device_id=dev, device_id_type=MESH,
-        )
-
-    def f_out(n, carry):
-        cols = pl.ds(pl.multiple_of(n * 256, 256), 256)
-        total = xin[0, :, cols].astype(F32) + nn(att[...], wo[:, cols])
-        res[0, :, cols] = total.astype(BF16)
-        return carry
-
-    lax.fori_loop(0, 4, f_out, 0)
-
-    @pl.when(z != 7)
-    def _():
-        for k in range(2):
-            pipe_copy(0, k, on_hbm, (up, seq_of(2 * c + k, y, x // 2)), x % 2, pf_ss, pf_rs).start()
-
-    def b_jacobian(i, carry):
+        ).start()
+
+    def f_leave(k):
+        @pl.when(z != 7)
+        def _():
+            pipe_start(0, k, on_hbm, (up, seq_of(f_source(k), y, x // 2)), x % 2, pf_ss, pf_rs)
+
+    f_result(0)
+    f_leave(0)
+    f_result(1)
+
+    def jacobian(t, h, k):
+        u = mixed[t, h, pl.ds(k * TILE, TILE)]
+        r = inv_rms(u)
+        unit = u * r
+        g = br[t, h, k].astype(F32)
+        back = r * (g - unit * jnp.mean(unit * g, axis=-1, keepdims=True))
+        gm[k, :, pl.ds(pl.multiple_of(t * D + h * HD, HD), HD)] = back.astype(BF16)
+
+    def b_queries(i, carry):
         h = ((x + ring_order(i // 2)) % 4) * 2 + i % 2
         landed(br.at[0, h], dq_rs.at[h])
-        landed(br.at[pl.ds(1, 2), h], dkv_rs.at[h])
-        for t in range(2):
-            u = mixed[t, h]
-            r = inv_rms(u)
-            unit = u * r
-            g = br[t, h].reshape(2 * TILE, HD).astype(F32)
-            back = r * (g - unit * jnp.mean(unit * g, axis=-1, keepdims=True))
-            gm[:, pl.ds(pl.multiple_of(t * D + h * HD, HD), HD)] = back.astype(BF16)
-        gm[:, pl.ds(pl.multiple_of(2 * D + h * HD, HD), HD)] = br[2, h].reshape(2 * TILE, HD)
-        return carry
-
-    lax.fori_loop(0, 8, b_jacobian, 0)
-
-    def b_normed(n, carry):
+        for k in range(2):
+            jacobian(0, h, k)
+        return carry
+
+    lax.fori_loop(0, 8, b_queries, 0)
+
+    def b_query_part(n, carry):
         cols = pl.ds(pl.multiple_of(n * 256, 256), 256)
-        gn[:, cols] = nn(gm[...], wq[:, cols])
-        return carry
-
-    lax.fori_loop(0, 4, b_normed, 0)
+        for k in range(2):
+            gn[k, :, cols] = nn(gm[k, :, :D], wq[:D, cols])
+        return carry
+
+    lax.fori_loop(0, 4, b_query_part, 0)
 
     for k in range(2):
+        for h in range(8):
+            landed(br.at[pl.ds(1, 2), h, k], dkv_rs.at[k, h])
+        if k == 1:
+            f_leave(1)
+
+        def b_keys(h, carry):
+            jacobian(1, h, k)
+            gm[k, :, pl.ds(pl.multiple_of(2 * D + h * HD, HD), HD)] = br[2, h, k]
+            return carry
+
+        lax.fori_loop(0, 8, b_keys, 0)
+
+        def b_normed(n, carry):
+            cols = pl.ds(pl.multiple_of(n * 256, 256), 256)
+            gn[k, :, cols] += nn(gm[k, :, D:], wq[D:, cols])
+            return carry
+
+        lax.fori_loop(0, 4, b_normed, 0)
         rows = pl.ds(k * TILE, TILE)
         u = xin[1, rows].astype(F32)
         r = inv_rms(u)
         unit = u * r
-        g = gn[rows]
+        g = gn[k]
         back = r * (g - unit * jnp.mean(unit * g, axis=-1, keepdims=True))
         res[1, rows] = (xin[2, rows].astype(F32) + back).astype(BF16)
 
         @pl.when(z != 0)
         def _():
-            pipe_copy(1, k, og_hbm, (down, seq_of(x, 2 * c + k, y // 2)), y % 2, pb_ss, pb_rs).start()
+            pipe_start(1, k, og_hbm, (down, seq_of(x, b_source(k), y // 2)), y % 2, pb_ss, pb_rs)
 
     for j in range(2):
         exchange_sent(0, j, True)
@@ -396,7 +447,8 @@
             landed(sb.at[h, pl.ds(0, 3)], b_ss.at[h])
             landed(sb.at[h, 3], d_ss.at[h])
             landed(bo.at[0, h], dq_ss.at[h])
-            landed(bo.at[pl.ds(1, 2), h], dkv_ss.at[h])
+            for k in range(2):
+                landed(bo.at[pl.ds(1, 2), h, k], dkv_ss.at[k, h])
 
         @pl.when(h != f_me)
         def _():
@@ -442,7 +494,9 @@
             pltpu.VMEM((HEADS, 3, 2, TILE, HD), BF16),
             pltpu.VMEM((HEADS, 4, 2, TILE, HD), BF16),
             pltpu.VMEM((3, GROUP + 1, TILE, HD), BF16),
-            pltpu.VMEM((4, GROUP + 1, TILE, HD), BF16),
+            pltpu.VMEM((3, GROUP + 1, TILE, HD), BF16),
+            pltpu.VMEM((GROUP + 1, TILE, HD), BF16),
+            pltpu.VMEM((GROUP, TILE, CAP * TILE), F32),
             pltpu.VMEM((GROUP + 1, CAP, TILE, HD), BF16),
             pltpu.VMEM((GROUP + 1, CAP, TILE, HD), BF16),
             pltpu.VMEM((HEADS, 2, TILE, HD), BF16),
@@ -450,13 +504,13 @@
             pltpu.VMEM((3, HEADS, 2, TILE, HD), BF16),
             pltpu.VMEM((3, HEADS, 2, TILE, HD), BF16),
             pltpu.VMEM((2 * TILE, D), BF16),
-            pltpu.VMEM((2 * TILE, 3 * D), BF16),
-            pltpu.VMEM((2 * TILE, D), F32),
+            pltpu.VMEM((2, TILE, 3 * D), BF16),
+            pltpu.VMEM((2, TILE, D), F32),
             pltpu.VMEM((2, 2 * TILE, D), BF16),
             pltpu.SMEM((2 * GROUP * LIST,), jnp.int32),
             dma((2,)), dma((3, 2)), dma((3, 2)),
             dma((8,)), dma((8,)), dma((8,)), dma((8,)), dma((8,)), dma((8,)),
-            dma((8,)), dma((8,)), dma((8,)), dma((8,)), dma((8,)), dma((8,)),
+            dma((8,)), dma((8,)), dma((8,)), dma((8,)), dma((2, 8)), dma((2, 8)),
             dma((2,)), dma((2,)), dma((2,)), dma((2,)),
         ],
         compiler_params=pltpu.CompilerParams(

time: 86.5 us -> 83.2 us (0.962)
  Pallas kernels: 83.4 us -> 79.8 us
    pallas_call x1, Pallas kernels: 83.4 us -> 79.8 us  [per_device(): pl.pallas_call(kernel, out_shape=(block, block), in_specs=[pl.BlockSpec(m...]
where the time goes in v1:
time: 83.2 us; the launch traced here: 82.6 us
  Pallas kernels  79.8 us (96%)
  other arithmetic  2.25 us (3%)
    pallas_call x1, Pallas kernels, per_device(): pl.pallas_call(kernel, out_shape=(block, block), in_specs=[pl.BlockSpec(m...  79.8 us
    select_n x1, other arithmetic, per_device(): jnp.where(z == lax.axis_size('pipe') - 1, nothing, back)  2.25 us

profile of v1, /device:TPU:91, one launch (start us, length us, event | category | flops | bytes accessed | tf_op | source)
XLA Modules:
  0.0 82.6 jit_solution(5051989633274401869)
XLA Ops:
  0.6 79.8 %shard_map.77 = (bf16[1,256,1024]{2,1,0:T(8,128)(2,1)}, bf16[1,256,1024]{2,1,0:T(8,128)(2,1)}) custom-call(s32[64]{0:T(128)} %tc_ref.1, bf16[1,256,1024]{2,1,0:T(8,128)(2,1)} %x_hbm.1, bf16[1,256,1024]{2,1,0:T(8,128)(2,1)} %xs_hbm.1, bf16[1,256,1024]{2,1,0:T(8,128)(2,1)} %g_hbm.1, bf16[1,3072,1024]{2,1,0:T(8,128)(2,1)} %wq_hbm.1, bf16[1,1024,1024]{2,1,0:T(8,128)(2,1)} %wo_hbm.1), custom_call_target="tpu_custom_call" | custom-call | tf_op jit(solution)/shard_map/pallas_call | solution.py:483
  80.4 2.2 %broadcast_select_fusion = (bf16[1,256,1024]{2,1,0:T(8,128)(2,1)}, bf16[1,256,1024]{2,1,0:T(8,128)(2,1)}) fusion(bf16[1,256,1024]{2,1,0:T(8,128)(2,1)} %get-tuple-element.5, pred[]{:T(512)S(6)} %eq.7, bf16[1,256,1024]{2,1,0:T(8,128)(2,1)} %get-tuple-element.4, pred[]{:T(512)S(6)} %eq.6), kind=kLoop, calls=%fused_computation | loop fusion | flops 524288 | bytes 2097154 | tf_op jit(solution)/shard_map/jit(_where)/select_n | solution.py:524

commit v2 on v1

--- a/solution.py
+++ b/solution.py
@@ -411,19 +411,21 @@
         if k == 1:
             f_leave(1)
 
-        def b_keys(h, carry):
-            jacobian(1, h, k)
-            gm[k, :, pl.ds(pl.multiple_of(2 * D + h * HD, HD), HD)] = br[2, h, k]
+        def b_keys(i, carry):
+            for n in range(4):
+                h = 4 * i + n
+                jacobian(1, h, k)
+                gm[k, :, pl.ds(pl.multiple_of(2 * D + h * HD, HD), HD)] = br[2, h, k]
             return carry
 
-        lax.fori_loop(0, 8, b_keys, 0)
+        lax.fori_loop(0, 2, b_keys, 0)
 
         def b_normed(n, carry):
-            cols = pl.ds(pl.multiple_of(n * 256, 256), 256)
+            cols = pl.ds(pl.multiple_of(n * 512, 512), 512)
             gn[k, :, cols] += nn(gm[k, :, D:], wq[D:, cols])
             return carry
 
-        lax.fori_loop(0, 4, b_normed, 0)
+        lax.fori_loop(0, 2, b_normed, 0)
         rows = pl.ds(k * TILE, TILE)
         u = xin[1, rows].astype(F32)
         r = inv_rms(u)

time: 83.2 us -> 81.8 us (0.983)
  Pallas kernels: 79.8 us -> 78.3 us
    pallas_call x1, Pallas kernels: 79.8 us -> 78.3 us  [per_device(): pl.pallas_call(kernel, out_shape=(block, block), in_specs=[pl.BlockSpec(m...]
where the time goes in v2:
time: 81.8 us; the launch traced here: 81.2 us
  Pallas kernels  78.3 us (96%)
  other arithmetic  2.25 us (3%)
    pallas_call x1, Pallas kernels, per_device(): pl.pallas_call(kernel, out_shape=(block, block), in_specs=[pl.BlockSpec(m...  78.3 us
    select_n x1, other arithmetic, per_device(): jnp.where(z == lax.axis_size('pipe') - 1, nothing, back)  2.25 us

profile of v2, /device:TPU:91, one launch (start us, length us, event | category | flops | bytes accessed | tf_op | source)
XLA Modules:
  0.0 81.2 jit_solution(3428755773837208976)
XLA Ops:
  0.6 78.3 %shard_map.77 = (bf16[1,256,1024]{2,1,0:T(8,128)(2,1)}, bf16[1,256,1024]{2,1,0:T(8,128)(2,1)}) custom-call(s32[64]{0:T(128)} %tc_ref.1, bf16[1,256,1024]{2,1,0:T(8,128)(2,1)} %x_hbm.1, bf16[1,256,1024]{2,1,0:T(8,128)(2,1)} %xs_hbm.1, bf16[1,256,1024]{2,1,0:T(8,128)(2,1)} %g_hbm.1, bf16[1,3072,1024]{2,1,0:T(8,128)(2,1)} %wq_hbm.1, bf16[1,1024,1024]{2,1,0:T(8,128)(2,1)} %wo_hbm.1), custom_call_target="tpu_custom_call" | custom-call | tf_op jit(solution)/shard_map/pallas_call | solution.py:485
  78.9 2.2 %broadcast_select_fusion = (bf16[1,256,1024]{2,1,0:T(8,128)(2,1)}, bf16[1,256,1024]{2,1,0:T(8,128)(2,1)}) fusion(bf16[1,256,1024]{2,1,0:T(8,128)(2,1)} %get-tuple-element.5, pred[]{:T(512)S(6)} %eq.7, bf16[1,256,1024]{2,1,0:T(8,128)(2,1)} %get-tuple-element.4, pred[]{:T(512)S(6)} %eq.6), kind=kLoop, calls=%fused_computation | loop fusion | flops 524288 | bytes 2097154 | tf_op jit(solution)/shard_map/jit(_where)/select_n | solution.py:526

commit v3 on v2

--- a/solution.py
+++ b/solution.py
@@ -356,12 +356,12 @@
         rows = pl.ds(k * TILE, TILE)
 
         def columns(n, carry):
-            cols = pl.ds(pl.multiple_of(n * 256, 256), 256)
+            cols = pl.ds(pl.multiple_of(n * 512, 512), 512)
             total = xin[0, rows, cols].astype(F32) + nn(att[rows], wo[:, cols])
             res[0, rows, cols] = total.astype(BF16)
             return carry
 
-        lax.fori_loop(0, 4, columns, 0)
+        lax.fori_loop(0, 2, columns, 0)
 
     def pipe_start(result, k, out, dev, slot, send_sem, recv_sem):
         pltpu.make_async_remote_copy(
@@ -388,22 +388,24 @@
         back = r * (g - unit * jnp.mean(unit * g, axis=-1, keepdims=True))
         gm[k, :, pl.ds(pl.multiple_of(t * D + h * HD, HD), HD)] = back.astype(BF16)
 
+    for h in range(8):
+        landed(br.at[0, h], dq_rs.at[h])
+
     def b_queries(i, carry):
-        h = ((x + ring_order(i // 2)) % 4) * 2 + i % 2
-        landed(br.at[0, h], dq_rs.at[h])
-        for k in range(2):
-            jacobian(0, h, k)
-        return carry
-
-    lax.fori_loop(0, 8, b_queries, 0)
+        for n in range(2):
+            for k in range(2):
+                jacobian(0, 2 * i + n, k)
+        return carry
+
+    lax.fori_loop(0, 4, b_queries, 0)
 
     def b_query_part(n, carry):
-        cols = pl.ds(pl.multiple_of(n * 256, 256), 256)
+        cols = pl.ds(pl.multiple_of(n * 512, 512), 512)
         for k in range(2):
             gn[k, :, cols] = nn(gm[k, :, :D], wq[:D, cols])
         return carry
 
-    lax.fori_loop(0, 4, b_query_part, 0)
+    lax.fori_loop(0, 2, b_query_part, 0)
 
     for k in range(2):
         for h in range(8):

time: 81.8 us -> 81.7 us (level)
  no operation moved by 1% of the time
where the time goes in v3:
time: 81.7 us; the launch traced here: 81.2 us
  Pallas kernels  78.3 us (96%)
  other arithmetic  2.25 us (3%)
    pallas_call x1, Pallas kernels, per_device(): pl.pallas_call(kernel, out_shape=(block, block), in_specs=[pl.BlockSpec(m...  78.3 us
    select_n x1, other arithmetic, per_device(): jnp.where(z == lax.axis_size('pipe') - 1, nothing, back)  2.25 us

profile of v3, /device:TPU:91, one launch (start us, length us, event | category | flops | bytes accessed | tf_op | source)
XLA Modules:
  0.0 81.2 jit_solution(11625627323243157941)
XLA Ops:
  0.6 78.3 %shard_map.77 = (bf16[1,256,1024]{2,1,0:T(8,128)(2,1)}, bf16[1,256,1024]{2,1,0:T(8,128)(2,1)}) custom-call(s32[64]{0:T(128)} %tc_ref.1, bf16[1,256,1024]{2,1,0:T(8,128)(2,1)} %x_hbm.1, bf16[1,256,1024]{2,1,0:T(8,128)(2,1)} %xs_hbm.1, bf16[1,256,1024]{2,1,0:T(8,128)(2,1)} %g_hbm.1, bf16[1,3072,1024]{2,1,0:T(8,128)(2,1)} %wq_hbm.1, bf16[1,1024,1024]{2,1,0:T(8,128)(2,1)} %wo_hbm.1), custom_call_target="tpu_custom_call" | custom-call | tf_op jit(solution)/shard_map/pallas_call | solution.py:487
  78.9 2.2 %broadcast_select_fusion = (bf16[1,256,1024]{2,1,0:T(8,128)(2,1)}, bf16[1,256,1024]{2,1,0:T(8,128)(2,1)}) fusion(bf16[1,256,1024]{2,1,0:T(8,128)(2,1)} %get-tuple-element.5, pred[]{:T(512)S(6)} %eq.7, bf16[1,256,1024]{2,1,0:T(8,128)(2,1)} %get-tuple-element.4, pred[]{:T(512)S(6)} %eq.6), kind=kLoop, calls=%fused_computation | loop fusion | flops 524288 | bytes 2097154 | tf_op jit(solution)/shard_map/jit(_where)/select_n | solution.py:528
